TPU v7x, 32 devices: a whole 2x2x4 slice. The times are simulated.
32 devices in a mesh: group: 8 (over y, x, core), fsdp: 4 (over z).
Axes of the slice: x: 2, y: 2, z: 4, core: 2. Of those that a mesh axis runs over, the one named last changes fastest.
Arguments:
- query_embeddings: bfloat16 [128, 4096], P(('group', 'fsdp')), may hold values from -4 to 4
- passage_embeddings: bfloat16 [128, 4096], P(('group', 'fsdp')), may hold values from -4 to 4
- positives: int32 [128], P(('group', 'fsdp')), may hold values from 0 to 127, each once
- logarithm_scale: float32 [], replicated, may hold values from 2.4 to 2.8
- residual_input: bfloat16 [32, 256, 4096], P(('group', 'fsdp')), may hold values from -6 to 6
- attention_head_outputs: bfloat16 [32, 256, 4096], P(('group', 'fsdp')), may hold values from -6 to 6
- output_weight: bfloat16 [4096, 4096], P('fsdp'), may hold values from -0.09375 to 0.09375
- adapter_down_weight: bfloat16 [4096, 16], replicated, may hold values from -0.09375 to 0.09375
- adapter_up_weight: bfloat16 [16, 4096], replicated, may hold values from -0.375 to 0.375
- final_norm_weight: float32 [4096], replicated, may hold values from 0.5 to 1.5
- lengths: int32 [32], P(('group', 'fsdp')), may hold values from 64 to 256
Outputs:
- loss: float32 [], replicated
- scale_grad: float32 [], replicated
- query_grad: float32 [128, 4096], P(('group', 'fsdp'))
- passage_grad: float32 [128, 4096], P(('group', 'fsdp'))
- attn_grad: bfloat16 [32, 256, 4096], P(('group', 'fsdp'))
- residual_grad: bfloat16 [32, 256, 4096], P(('group', 'fsdp'))
- lora_down_grad: float32 [4096, 16], replicated
- lora_up_grad: float32 [16, 4096], replicated
All inputs are finite; a program needn't handle non-finite values.
Results may differ from a plain program's by a relative error of at most 0.01.
Values may be sent and summed in bfloat16 or wider, within the bound.
A program may use at most 128 MiB of HBM per device.

v0:
```python
import jax
import jax.numpy as jnp
from jax import lax
from jax.sharding import PartitionSpec as P

grad_scale = 512.0
adapter_scale = 2.0
epsilon = 1e-05
contract_rows = (((0,), (0,)), ((), ()))
contracted_columns = (((1,), (1,)), ((), ()))


def on_device(
    query_embeddings,
    passage_embeddings,
    positives,
    logarithm_scale,
    residual_input,
    attention_head_outputs,
    output_weight,
    adapter_down_weight,
    adapter_up_weight,
    final_norm_weight,
    lengths,
):
    device_count = lax.axis_size(("group", "fsdp"))
    own_index = lax.axis_index(("group", "fsdp"))
    q_count, model_width = query_embeddings.shape
    total_queries = q_count * device_count
    logit_scale = jnp.exp(logarithm_scale)
    seq_here, seq_len, _ = residual_input.shape
    heads_width = attention_head_outputs.shape[2]
    token_rows = attention_head_outputs.reshape(-1, heads_width)
    my_columns = lax.all_to_all(token_rows, "fsdp", split_axis=1, concat_axis=0, tiled=True)
    projected_output = lax.psum_scatter(
        jnp.dot(my_columns, output_weight, preferred_element_type=jnp.float32).astype(jnp.bfloat16),
        "fsdp",
        scatter_dimension=0,
        tiled=True,
    ).astype(jnp.float32)
    reduced_activation = jnp.dot(
        token_rows, adapter_down_weight, preferred_element_type=jnp.float32
    ).astype(jnp.bfloat16)
    hidden_state = (
        residual_input.reshape(-1, model_width).astype(jnp.float32)
        + projected_output
        + adapter_scale
        * jnp.dot(reduced_activation, adapter_up_weight, preferred_element_type=jnp.float32)
    )
    own_passages = own_index * q_count + jnp.arange(q_count, dtype=jnp.int32)
    zero_rows = jnp.zeros((q_count,), jnp.float32)
    zero_block = jnp.zeros((q_count, model_width), jnp.float32)
    block_rows = lax.all_gather(passage_embeddings, ("group", "fsdp"), axis=0, tiled=True)
    row_max = jnp.full((q_count,), -jnp.inf, jnp.float32)
    row_sum = zero_rows
    weighted = zero_block
    product = zero_rows
    logits = logit_scale * lax.dot_general(
        query_embeddings, block_rows, contracted_columns, preferred_element_type=jnp.float32
    )
    column = jnp.arange(block_rows.shape[0], dtype=jnp.int32)
    pos_hit = column[None, :] == positives[:, None]
    pos_logit = jnp.sum(jnp.where(pos_hit, logits, 0.0), axis=1)
    new_max = jnp.max(logits, axis=1)
    rescale = jnp.exp(row_max - new_max)
    exp_terms = jnp.exp(logits - new_max[:, None])
    row_sum = row_sum * rescale + jnp.sum(exp_terms, axis=1)
    product = product * rescale + jnp.sum(exp_terms * logits, axis=1)
    weighted = weighted * rescale[:, None] + jnp.dot(
        exp_terms.astype(jnp.bfloat16), block_rows, preferred_element_type=jnp.float32
    )
    hit_rows = jnp.dot(pos_hit.astype(jnp.bfloat16), block_rows, preferred_element_type=jnp.float32)
    row_max, row_sum, weighted, hit_rows, product, pos_logit = (
        new_max,
        row_sum,
        weighted,
        hit_rows,
        product,
        pos_logit,
    )
    log_norm = row_max + jnp.log(row_sum)
    loss_part = jnp.sum(log_norm - pos_logit)
    scale_part = jnp.sum(product / row_sum - pos_logit)
    query_grad = logit_scale * (weighted / row_sum[:, None] - hit_rows)
    norm_all, pos_all = (
        lax.all_gather(log_norm, ("group", "fsdp"), axis=0, tiled=True),
        lax.all_gather(positives, ("group", "fsdp"), axis=0, tiled=True),
    )
    block_rows = lax.all_gather(query_embeddings, ("group", "fsdp"), axis=0, tiled=True)
    logits = logit_scale * lax.dot_general(
        block_rows, passage_embeddings, contracted_columns, preferred_element_type=jnp.float32
    )
    block_weights = jnp.exp(logits - norm_all[:, None]).astype(jnp.bfloat16)
    block_hits = (pos_all[:, None] == own_passages[None, :]).astype(jnp.bfloat16)
    summed = lax.dot_general(
        block_weights, block_rows, contract_rows, preferred_element_type=jnp.float32
    )
    passage_grad = logit_scale * (
        summed
        - lax.dot_general(block_hits, block_rows, contract_rows, preferred_element_type=jnp.float32)
    )
    row_grads = query_grad[:seq_here]
    position = jnp.arange(seq_len, dtype=jnp.int32)
    weight = (
        grad_scale
        * (position[None, :] < lengths[:, None]).astype(jnp.float32)
        / lengths[:, None].astype(jnp.float32)
    )
    gained = (
        weight[:, :, None] * row_grads[:, None, :] * final_norm_weight[None, None, :]
    ).reshape(-1, model_width)
    inv_rms = lax.rsqrt(jnp.mean(hidden_state * hidden_state, axis=1) + epsilon)
    hidden_grad = (
        inv_rms[:, None] * gained
        - hidden_state
        * (inv_rms * inv_rms * inv_rms * jnp.mean(gained * hidden_state, axis=1))[:, None]
    )
    gradient_portion = hidden_grad.astype(jnp.bfloat16)
    reduced_gradient = (
        adapter_scale
        * lax.dot_general(
            gradient_portion,
            adapter_up_weight,
            contracted_columns,
            preferred_element_type=jnp.float32,
        )
    ).astype(jnp.bfloat16)
    partial_back = lax.dot_general(
        lax.all_gather(gradient_portion, "fsdp", axis=0, tiled=True),
        output_weight,
        contracted_columns,
        preferred_element_type=jnp.float32,
    )
    main_back = lax.all_to_all(
        partial_back.astype(jnp.bfloat16), "fsdp", split_axis=0, concat_axis=1, tiled=True
    ).astype(partial_back.dtype)
    head_gradient = (
        main_back
        + lax.dot_general(
            reduced_gradient,
            adapter_down_weight,
            contracted_columns,
            preferred_element_type=jnp.float32,
        )
    ).astype(jnp.bfloat16)
    down_part = lax.dot_general(
        token_rows, reduced_gradient, contract_rows, preferred_element_type=jnp.float32
    )
    up_weight_partial = adapter_scale * lax.dot_general(
        reduced_activation, gradient_portion, contract_rows, preferred_element_type=jnp.float32
    )
    loss_total, scale_total = lax.psum((loss_part, scale_part), ("group", "fsdp"))
    down_total, up_total = lax.psum((down_part, up_weight_partial), ("group", "fsdp"))
    seqs_all = seq_here * device_count
    loss = loss_total / total_queries
    scale_grad = scale_total / total_queries
    attn_grad = head_gradient.reshape(seq_here, seq_len, heads_width)
    residual_grad = gradient_portion.reshape(seq_here, seq_len, model_width)
    return (
        loss,
        scale_grad,
        query_grad,
        passage_grad,
        attn_grad,
        residual_grad,
        down_total / seqs_all,
        up_total / seqs_all,
    )


def solution(mesh):
    placed = (
        P(("group", "fsdp"), None),
        P(("group", "fsdp"), None),
        P(("group", "fsdp")),
        P(),
        P(("group", "fsdp"), None, None),
        P(("group", "fsdp"), None, None),
        P("fsdp", None),
        P(),
        P(),
        P(),
        P(("group", "fsdp")),
    )
    return jax.shard_map(
        on_device,
        mesh=mesh,
        in_specs=placed,
        out_specs=(
            P(),
            P(),
            P(("group", "fsdp"), None),
            P(("group", "fsdp"), None),
            P(("group", "fsdp"), None, None),
            P(("group", "fsdp"), None, None),
            P(),
            P(),
        ),
        check_vma=False,
    )
```

profile of v0, /device:TPU:1, one launch (start us, length us, event | category | flops | bytes accessed | tf_op | source)
XLA Modules:
  0.0 597.1 jit_solution(17894894612356255882)
XLA Ops:
  8.0 4.1 copy.24
  12.1 5.4 all-to-all-start
  18.3 47.6 %all-to-all-done = bf16[256,4,1024]{0,2,1:T(8,128)(2,1)S(1)} async-done(((bf16[256,4,1024]{0,2,1:T(8,128)(2,1)}), bf16[256,4,1024]{0,2,1:T(8,128)(2,1)S(1)}, u32[]{:S(2)}, u32[]{:S(2)}) %all-to-all-start) | async-done | bytes 2097184 | tf_op jit(solution)/shard_map/all_to_all | solution.py:34
  65.9 2.4 copy.25
  68.3 14.7 %convolution_convert_fusion = bf16[1024,4096]{1,0:T(8,128)(2,1)} fusion(bf16[1024,1024]{1,0:T(8,128)(2,1)} %bitcast.56, bf16[1024,4096]{1,0:T(8,128)(2,1)} %param.17), kind=kOutput, calls=%fused_computation | convolution fusion | flops 8594128896 | bytes 18874368 | tf_op jit(solution)/shard_map/dot_general | solution.py:36
  85.9 31.6 %all-gather.8.cloned.1.call-done = bf16[32,4,4096]{2,1,0:T(4,128)(2,1)} async-done(((bf16[1,4,4096]{2,1,0:T(4,128)(2,1)}), bf16[32,4,4096]{2,1,0:T(4,128)(2,1)}) %all-gather.8.cloned.1.call-update) | async-done | bytes 1048592 | tf_op jit(solution)/shard_map/all_gather | solution.py:53
  121.0 107.5 %reduce-scatter.2.cloned.1.call-done = bf16[256,4096]{1,0:T(8,128)(2,1)} async-done(((bf16[1024,4096]{1,0:T(8,128)(2,1)}), bf16[256,4096]{1,0:T(8,128)(2,1)}) %reduce-scatter.2.cloned.1.call-update) | async-done | bytes 2097168 | tf_op jit(solution)/shard_map/reduce_scatter | solution.py:35
  228.5 4.0 multiply_reduce_fusion.1
  232.6 1.9 copy-done.5
  234.5 2.5 subtract_convert_fusion
  237.3 42.2 %all-reduce.1 = s32[128]{0:T(128)} all-reduce(s32[128]{0:T(128)S(1)} %dynamic-update-slice.1), channel_id=1, replica_groups=mesh['group'=8,'fsdp'=4] {'group','fsdp'}, use_global_device_ids=true, to_apply=%add.1 | all-reduce | flops 128 | bytes 1024
  280.0 46.6 %all-reduce.2 = (f32[]{:T(128)}, f32[]{:T(128)}, f32[128]{0:T(128)}) all-reduce(f32[]{:T(128)} %get-tuple-element.14, f32[]{:T(128)} %get-tuple-element.13, f32[128]{0:T(128)S(1)} %get-tuple-element.23), channel_id=1, replica_groups=mesh['group'=8,'fsdp'=4] {'group','fsdp'}, use_global_device_ids=true, to_apply=%region_4.5 | all-reduce | flops 130 | bytes 1040 | tf_op jit(solution)/shard_map/psum | solution.py:152
  327.9 1.4 reshape.133
  329.2 1.5 fusion.16
  330.8 1.7 fusion.3
  334.2 70.9 %all-gather.6.cloned.1.call-done = bf16[1024,4096]{1,0:T(8,128)(2,1)} async-done(((bf16[256,4096]{1,0:T(8,128)(2,1)}), bf16[1024,4096]{1,0:T(8,128)(2,1)}) %all-gather.6.cloned.1.call-update) | async-done | bytes 8388624 | tf_op jit(solution)/shard_map/all_gather | solution.py:129
  405.1 14.7 %convolution_convert_fusion.1 = bf16[1024,1024]{1,0:T(8,128)(2,1)} fusion(bf16[1024,4096]{1,0:T(8,128)(2,1)} %all-gather.6.cloned.1.call-done, bf16[1024,4096]{1,0:T(8,128)(2,1)} %param.17), kind=kOutput, calls=%fused_computation.23 | convolution fusion | flops 8590983168 | bytes 18874368 | tf_op jit(solution)/shard_map/dot_general | solution.py:128
  419.8 4.6 all-to-all-start.1
  425.6 4.6 fusion.54
  430.2 149.5 %all-reduce.6.cloned.1.call-done = (f32[4096,16]{0,1:T(8,128)}, f32[16,4096]{1,0:T(8,128)}) async-done(((f32[4096,16]{0,1:T(8,128)}, f32[16,4096]{1,0:T(8,128)}), (f32[4096,16]{0,1:T(8,128)}, f32[16,4096]{1,0:T(8,128)})) %all-reduce.6.cloned.1.call-update) | async-done | bytes 524304 | tf_op jit(solution)/shard_map/psum | solution.py:153
  579.7 1.7 broadcast_multiply_fusion
  581.4 1.7 broadcast_multiply_fusion.1
  583.0 2.0 convert_bitcast_fusion
  585.7 2.1 fusion.2
  (57 shorter events, 9.9 us)
Async XLA Ops:
  8.0 220.5 %copy-start = (bf16[16,4096]{1,0:T(8,128)(2,1)S(1)}, bf16[16,4096]{1,0:T(8,128)(2,1)}, u32[]{:S(2)}) copy-start(bf16[16,4096]{1,0:T(8,128)(2,1)} %param.19) | copy-start | bytes 393220
  12.1 53.8 %all-to-all-start = ((bf16[256,4,1024]{0,2,1:T(8,128)(2,1)}), bf16[256,4,1024]{0,2,1:T(8,128)(2,1)S(1)}, u32[]{:S(2)}, u32[]{:S(2)}) async-start(bf16[256,4,1024]{0,2,1:T(8,128)(2,1)} %bitcast.54), calls=%async_computation | async-start | bytes 4194304 | tf_op jit(solution)/shard_map/all_to_all | solution.py:34
  17.5 100.0 %all-gather.8.cloned.1.call-start = ((), (), s32[]{:S(2)}) async-start(), calls=%async_computation.5 | async-start | bytes 1081344 | tf_op jit(solution)/shard_map/all_gather | solution.py:53
  18.3 210.2 %reduce-scatter.2.cloned.1.call-start = ((), (), s32[]{:S(2)}) async-start(), calls=%async_computation.3 | async-start | bytes 10485760 | tf_op jit(solution)/shard_map/reduce_scatter | solution.py:35
  83.0 2.2 copy-start.3
  83.0 2.2 copy-start.6
  83.0 35.8 %copy-start.8 = (bf16[4,4096]{1,0:T(4,128)(2,1)S(1)}, bf16[4,4096]{1,0:T(4,128)(2,1)}, u32[]{:S(2)}) copy-start(bf16[4,4096]{1,0:T(4,128)(2,1)} %param.11) | copy-start | bytes 98308
  83.0 36.3 %copy-start.13 = (s32[4]{0:T(128)S(1)}, s32[4]{0:T(128)}, u32[]{:S(2)}) copy-start(s32[4]{0:T(128)} %param.13) | copy-start | bytes 52
  83.1 145.4 %copy-start.10 = (f32[4096]{0:T(1024)S(1)}, f32[4096]{0:T(1024)}, u32[]{:S(2)}) copy-start(f32[4096]{0:T(1024)} %param.20) | copy-start | bytes 49156
  83.1 244.8 %all-gather.10.cloned.1.call-start = ((), (), s32[]{:S(2)}) async-start(), calls=%async_computation.6 | async-start | bytes 1081344 | tf_op jit(solution)/shard_map/all_gather | solution.py:89
  83.8 321.3 %all-gather.6.cloned.1.call-start = ((), (), s32[]{:S(2)}) async-start(), calls=%async_computation.4 | async-start | bytes 10485760 | tf_op jit(solution)/shard_map/all_gather | solution.py:129
  120.9 111.6 %copy-start.9 = (f32[4,4096]{1,0:T(4,128)}, f32[4,4096]{1,0:T(4,128)S(1)}, u32[]{:S(2)}) copy-start(f32[4,4096]{1,0:T(4,128)S(1)} %fusion.4) | copy-start | bytes 196612
  232.5 2.0 copy-start.5
  232.6 4.4 copy-start.11
  234.5 94.7 %copy-start.7 = (bf16[4,4096]{1,0:T(4,128)(2,1)S(1)}, bf16[4,4096]{1,0:T(4,128)(2,1)}, u32[]{:S(2)}) copy-start(bf16[4,4096]{1,0:T(4,128)(2,1)} %param.12) | copy-start | bytes 98308
  237.0 95.5 %copy-start.2 = (bf16[256,4096]{1,0:T(8,128)(2,1)S(1)}, bf16[256,4096]{1,0:T(8,128)(2,1)}, u32[]{:S(2)}) copy-start(bf16[256,4096]{1,0:T(8,128)(2,1)} %subtract_convert_fusion) | copy-start | bytes 6291460
  419.8 4.6 copy-start.4
  419.8 5.8 copy-start.12
  419.8 163.2 %all-to-all-start.1 = ((bf16[4,256,1024]{2,1,0:T(8,128)(2,1)}), bf16[4,256,1024]{2,1,0:T(8,128)(2,1)}, u32[]{:S(2)}, u32[]{:S(2)}) async-start(bf16[4,256,1024]{2,1,0:T(8,128)(2,1)} %bitcast.55), calls=%async_computation.2 | async-start | bytes 4194304 | tf_op jit(solution)/shard_map/all_to_all | solution.py:134
  424.4 155.3 %all-reduce.6.cloned.1.call-start = ((), (), s32[]{:S(2)}) async-start(), calls=%async_computation.7 | async-start | bytes 1048576 | tf_op jit(solution)/shard_map/psum | solution.py:153
  585.1 2.7 copy-start.1
Sparse Core Ops, SparseCore 0:
  21.4 96.1 all-gather.7
  120.5 132.7 all-gather.9
  255.4 149.6 all-gather.5
  430.9 148.7 all-reduce.5
Sparse Core Ops, SparseCore 1:
  83.1 145.3 reduce-scatter.1
where the time goes:
time: 599 us; the launch traced here: 597 us
  waiting for transfers between devices  409 us (68%)
  blocking collectives  88.8 us (15%)
  matrix products  43.3 us (7%)
  between operations  20.4 us (3%)
  other arithmetic  14 us (2%)
  local copies, waits for them, and re-layouts  12 us (2%)
  starting transfers between devices  10.2 us (2%)
    psum x1, waiting for transfers between devices, on_device(): lax.psum((down_part, up_weight_partial), ('group', 'fsdp'))  149 us
    reduce_scatter x1, waiting for transfers between devices, on_device(): lax.psum_scatter(jnp.dot(my_columns, output_weight, preferred_element_typ...  108 us
    all_gather x1, waiting for transfers between devices, on_device(): lax.all_gather(gradient_portion, 'fsdp', axis=0, tiled=True)  70.9 us
    all_to_all x1, waiting for transfers between devices, on_device(): lax.all_to_all(token_rows, 'fsdp', split_axis=1, concat_axis=0, tiled=True)  47.6 us
    psum x1, blocking collectives, on_device(): lax.psum((loss_part, scale_part), ('group', 'fsdp'))  46.6 us
    unnamed x1, blocking collectives  42.2 us
    all_gather x1, waiting for transfers between devices, on_device(): lax.all_gather(passage_embeddings, ('group', 'fsdp'), axis=0, tiled=True)  31.6 us
    dot_general x1, matrix products, on_device(): jnp.dot(my_columns, output_weight, preferred_element_type=jnp.float32)  14.7 us
  transfers between devices with their start and end apart: 7, of which 5 were waited for; matrix products, arithmetic and copies ran while one was open for 7% of the time, Pallas kernels for 0%

commit v1 on v0

v1 whole, which is shorter than its diff:
```python
import functools

import jax
import jax.numpy as jnp
from jax import lax
from jax.experimental import pallas as pl
from jax.experimental.pallas import tpu as pltpu
from jax.sharding import PartitionSpec as P

grad_scale = 512.0
adapter_scale = 2.0
epsilon = 1e-05
contract_rows = (((0,), (0,)), ((), ()))
contracted_columns = (((1,), (1,)), ((), ()))
MESH = pl.DeviceIdType.MESH
code_base = 256


def remote(src, dst, send, recv, target):
    return pltpu.make_async_remote_copy(
        src_ref=src, dst_ref=dst, send_sem=send, recv_sem=recv, device_id=target, device_id_type=MESH
    )


def greet(targets):
    barrier = pltpu.get_barrier_semaphore()
    for target in targets:
        pl.semaphore_signal(barrier, inc=1, device_id=target, device_id_type=MESH)
    pl.semaphore_wait(barrier, len(targets))


def gather_kernel(
    groups, shards, own_w, own_pair, w_all, pair_all,
    local_sem, z_send, z_recv, pz_send, pz_recv,
    ring_send, ring_recv, sib_send, sib_recv,
):
    g = lax.axis_index("group")
    f = lax.axis_index("fsdp")
    core = lax.rem(g, 2)
    chip = lax.div(g, 2)
    chips = groups // 2
    half_ring = chips // 2
    sibling = (g + 1 - 2 * core, f)
    column, line = lax.rem(chip, 2), lax.div(chip, 2)
    place = column * (chips - 1 - line) + (1 - column) * line
    rows = own_w.shape[0]
    part = rows // groups
    half = part // 2

    def member(position):
        position = lax.rem(position + 2 * chips, chips)
        back = lax.div(position, half_ring)
        where = (1 - back) * 2 * position + back * (2 * (chips - 1 - position) + 1)
        return 2 * where + core

    neighbours = ((member(place + 1), f), (member(place - 1), f))
    greet([(g, lax.rem(f + k, shards)) for k in range(1, shards)] + list(neighbours) + [sibling])

    def piece(block, owner):
        return w_all.at[pl.ds(pl.multiple_of(block * rows + owner * part, 16), part)]

    def half_piece(block, owner, way):
        return w_all.at[pl.ds(pl.multiple_of(block * rows + owner * part + way * half, 16), half)]

    def z_copy(k, side):
        step = 1 - 2 * side
        block = f - step * (k - 1)
        here = own_w.at[pl.ds(pl.multiple_of(g * part, 16), part)] if k == 1 else piece(block, g)
        there = (block >= 0) & (block < shards) & (f + step >= 0) & (f + step < shards)
        return there, remote(
            here, piece(block, g), z_send.at[side, k - 1], z_recv.at[side, k - 1], (g, f + step)
        )

    def z_start(k):
        for side in (0, 1):
            there, copy = z_copy(k, side)

            @pl.when(there)
            def _():
                copy.start()

    def z_wait(k):
        for side in (0, 1):
            block = f - (1 - 2 * side) * k

            @pl.when((block >= 0) & (block < shards))
            def _():
                remote(
                    piece(block, g), piece(block, g), z_send.at[side, k - 1], z_recv.at[side, k - 1], sibling
                ).wait_recv()

    z_start(1)
    keep_w = pltpu.make_async_copy(
        own_w, w_all.at[pl.ds(pl.multiple_of(f * rows, 16), rows)], local_sem.at[0]
    )
    keep_pair = pltpu.make_async_copy(own_pair, pair_all.at[g, f], local_sem.at[1])
    keep_pair.start()
    pair_copies = [
        remote(own_pair, pair_all.at[g, f], pz_send.at[k], pz_recv.at[k], (g, lax.rem(f + k, shards)))
        for k in range(1, shards)
    ]
    for copy in pair_copies:
        copy.start()
    keep_w.start()
    keep_pair.wait()
    for k in range(1, shards):
        source = lax.rem(f + shards - k, shards)
        remote(own_pair, pair_all.at[g, source], pz_send.at[k], pz_recv.at[k], sibling).wait_recv()

    def ring(slot, whole, halves):
        pieces = []
        own = remote(whole, whole, sib_send.at[slot, chips - 1, 0], sib_recv.at[slot, chips - 1, 0], sibling)
        own.start()
        for h in range(1, chips):
            for way in (0, 1):
                step = 1 - 2 * way
                src = halves(member(place - step * (h - 1)), way)
                remote(
                    src, src, ring_send.at[slot, h - 1, way], ring_recv.at[slot, h - 1, way], neighbours[way]
                ).start()
            for way in (0, 1):
                step = 1 - 2 * way
                got = halves(member(place - step * h), way)
                remote(
                    got, got, ring_send.at[slot, h - 1, way], ring_recv.at[slot, h - 1, way], neighbours[way]
                ).wait_recv()
                remote(
                    got, got, sib_send.at[slot, h - 1, way], sib_recv.at[slot, h - 1, way], sibling
                ).start()

    def ring_finish(slot, whole, halves, other_whole, other_halves):
        own = remote(whole, other_whole, sib_send.at[slot, chips - 1, 0], sib_recv.at[slot, chips - 1, 0], sibling)
        own.wait_send()
        own.wait_recv()
        for h in range(1, chips):
            for way in (0, 1):
                step = 1 - 2 * way
                sent = halves(member(place - step * (h - 1)), way)
                remote(
                    sent, sent, ring_send.at[slot, h - 1, way], ring_recv.at[slot, h - 1, way], neighbours[way]
                ).wait_send()
                got = halves(member(place - step * h), way)
                other = other_halves(member(place - step * h), way)
                handed = remote(
                    got, other, sib_send.at[slot, h - 1, way], sib_recv.at[slot, h - 1, way], sibling
                )
                handed.wait_send()
                handed.wait_recv()

    middle = shards // 2

    def pair_half(owner, way):
        return pair_all.at[owner, pl.ds(way * middle, middle)]

    def flip(owner):
        return owner + 1 - 2 * core

    ring(shards, pair_all.at[g], pair_half)

    def w_ring(block):
        ring(block, piece(block, g), lambda owner, way: half_piece(block, owner, way))

    def w_finish(block):
        ring_finish(
            block,
            piece(block, g),
            lambda owner, way: half_piece(block, owner, way),
            piece(block, flip(g)),
            lambda owner, way: half_piece(block, flip(owner), way),
        )

    def blocks(k):
        low = (f - k >= 0).astype(jnp.int32)
        high = (f + k < shards).astype(jnp.int32)
        first = low * (f - k) + (1 - low) * (f + k)
        return ((low + high > 0, first), (low + high > 1, f + k))

    z_wait(1)
    if shards > 2:
        z_start(2)
    for k in range(1, shards):
        first, second = blocks(k)

        @pl.when(first[0])
        def _():
            w_ring(first[1])

        if k + 1 < shards:
            z_wait(k + 1)
        if k + 2 < shards:
            z_start(k + 2)

        @pl.when(second[0])
        def _():
            w_ring(second[1])

    ring_finish(
        shards, pair_all.at[g], pair_half, pair_all.at[flip(g)], lambda owner, way: pair_half(flip(owner), way)
    )
    for k in range(1, shards):
        for there, block in blocks(k):

            @pl.when(there)
            def _():
                w_finish(block)

        for side in (0, 1):
            there, copy = z_copy(k, side)

            @pl.when(there)
            def _():
                copy.wait_send()

    for copy in pair_copies:
        copy.wait_send()
    keep_w.wait()


def gather_all(groups, shards, own_w, own_pair):
    rows, width = own_w.shape
    chips = groups // 2
    any_space = pl.BlockSpec(memory_space=pl.ANY)
    dma = pltpu.SemaphoreType.DMA
    return pl.pallas_call(
        functools.partial(gather_kernel, groups, shards),
        out_shape=(
            jax.ShapeDtypeStruct((shards * rows, width), own_w.dtype),
            jax.ShapeDtypeStruct((groups, shards) + own_pair.shape, own_pair.dtype),
        ),
        in_specs=[any_space, any_space],
        out_specs=(any_space, any_space),
        scratch_shapes=[
            dma((2,)),
            dma((2, shards)),
            dma((2, shards)),
            dma((shards,)),
            dma((shards,)),
            dma((shards + 1, chips, 2)),
            dma((shards + 1, chips, 2)),
            dma((shards + 1, chips, 2)),
            dma((shards + 1, chips, 2)),
        ],
        compiler_params=pltpu.CompilerParams(collective_id=0, has_side_effects=True),
        name="gather_all",
    )(own_w, own_pair)


def sum_kernel(groups, shards, part, out, in_group, in_shard, mine, total, sem_send, sem_recv):
    g = lax.axis_index("group")
    f = lax.axis_index("fsdp")
    group_to = [(lax.rem(g + k, groups), f) for k in range(1, groups)]
    shard_to = [(g, lax.rem(f + k, shards)) for k in range(1, shards)]
    greet(group_to + shard_to)

    def stage(index, copies):
        for copy in copies:
            copy.start()
        return copies

    first = stage(0, [
        remote(part.at[group_to[k - 1][0]], in_group.at[k], sem_send.at[0, k], sem_recv.at[0, k], group_to[k - 1])
        for k in range(1, groups)
    ])
    total_here = part[g]
    for k, copy in enumerate(first):
        copy.wait_recv()
        total_here = total_here + in_group[k + 1]
    mine[...] = total_here
    second = stage(1, [
        remote(mine.at[shard_to[k - 1][1]], in_shard.at[k], sem_send.at[1, k], sem_recv.at[1, k], shard_to[k - 1])
        for k in range(1, shards)
    ])
    total_here = mine[f]
    for k, copy in enumerate(second):
        copy.wait_recv()
        total_here = total_here + in_shard[k + 1]
    total[g, f] = total_here
    third = stage(2, [
        remote(total.at[g, f], total.at[g, f], sem_send.at[2, k], sem_recv.at[2, k], shard_to[k - 1])
        for k in range(1, shards)
    ])
    for k in range(1, shards):
        source = lax.rem(f + shards - k, shards)
        remote(
            total.at[g, f], total.at[g, source], sem_send.at[2, k], sem_recv.at[2, k], shard_to[k - 1]
        ).wait_recv()
    fourth = stage(3, [
        remote(total.at[g], total.at[g], sem_send.at[3, k], sem_recv.at[3, k], group_to[k - 1])
        for k in range(1, groups)
    ])
    for k in range(1, groups):
        source = lax.rem(g + groups - k, groups)
        remote(
            total.at[g], total.at[source], sem_send.at[3, k], sem_recv.at[3, k], group_to[k - 1]
        ).wait_recv()
    out[...] = total[...]
    for copy in first + second + third + fourth:
        copy.wait_send()


def sum_all(groups, shards, part):
    rows, lanes = part.shape[2:]
    vmem = pl.BlockSpec(memory_space=pltpu.VMEM)
    most = max(groups, shards)
    return pl.pallas_call(
        functools.partial(sum_kernel, groups, shards),
        out_shape=jax.ShapeDtypeStruct(part.shape, part.dtype),
        in_specs=[vmem],
        out_specs=vmem,
        scratch_shapes=[
            pltpu.VMEM((groups, shards, rows, lanes), part.dtype),
            pltpu.VMEM((shards, rows, lanes), part.dtype),
            pltpu.VMEM((shards, rows, lanes), part.dtype),
            pltpu.VMEM(part.shape, part.dtype),
            pltpu.SemaphoreType.DMA((4, most)),
            pltpu.SemaphoreType.DMA((4, most)),
        ],
        compiler_params=pltpu.CompilerParams(collective_id=1, has_side_effects=True),
        name="sum_all",
    )(part)


def on_device(
    groups,
    shards,
    query_embeddings,
    passage_embeddings,
    positives,
    logarithm_scale,
    residual_input,
    attention_head_outputs,
    output_weight,
    adapter_down_weight,
    adapter_up_weight,
    final_norm_weight,
    lengths,
):
    device_count = groups * shards
    own_index = lax.axis_index(("group", "fsdp"))
    q_count, model_width = query_embeddings.shape
    total_queries = q_count * device_count
    logit_scale = jnp.exp(logarithm_scale)
    seq_here, seq_len, _ = residual_input.shape
    heads_width = attention_head_outputs.shape[2]
    rank = adapter_up_weight.shape[0]
    token_rows = attention_head_outputs.reshape(-1, heads_width)

    packed_width = q_count * model_width // 8
    code = jnp.concatenate([positives // code_base, positives % code_base]).astype(jnp.bfloat16)
    code = jnp.broadcast_to(jnp.pad(code, (0, 128 - 2 * q_count))[None, :], (16, 128))
    own_pair = jnp.concatenate(
        [
            jnp.concatenate(
                [query_embeddings.reshape(8, packed_width), passage_embeddings.reshape(8, packed_width)], axis=0
            ),
            code,
        ],
        axis=1,
    )
    full_weight, pairs = gather_all(groups, shards, output_weight, own_pair)
    pairs = pairs.reshape(device_count, 16, packed_width + 128)
    queries = pairs[:, :8, :packed_width].reshape(total_queries, model_width)
    passages = pairs[:, 8:, :packed_width].reshape(total_queries, model_width)
    codes = pairs[:, 0, packed_width : packed_width + 2 * q_count].astype(jnp.int32)
    pos_all = (codes[:, :q_count] * code_base + codes[:, q_count:]).reshape(total_queries)

    logits = logit_scale * lax.dot_general(
        queries, passages, contracted_columns, preferred_element_type=jnp.float32
    )
    hits = jnp.arange(total_queries, dtype=jnp.int32)[None, :] == pos_all[:, None]
    row_max = jnp.max(logits, axis=1)
    log_norm = row_max + jnp.log(jnp.sum(jnp.exp(logits - row_max[:, None]), axis=1))
    pos_logit = jnp.sum(jnp.where(hits, logits, 0.0), axis=1)
    weights = jnp.exp(logits - log_norm[:, None])
    loss = jnp.mean(log_norm - pos_logit)
    scale_grad = jnp.mean(jnp.sum(weights * logits, axis=1) - pos_logit)
    weight_half = weights.astype(jnp.bfloat16)
    hot_half = hits.astype(jnp.bfloat16)
    first_own = own_index * q_count
    own_rows = jnp.concatenate(
        [
            lax.dynamic_slice_in_dim(weight_half, first_own, q_count, 0),
            lax.dynamic_slice_in_dim(hot_half, first_own, q_count, 0),
        ],
        axis=0,
    )
    own_columns = jnp.concatenate(
        [
            lax.dynamic_slice_in_dim(weight_half, first_own, q_count, 1),
            lax.dynamic_slice_in_dim(hot_half, first_own, q_count, 1),
        ],
        axis=1,
    )
    by_query = jnp.dot(own_rows, passages, preferred_element_type=jnp.float32)
    query_grad = logit_scale * (by_query[:q_count] - by_query[q_count:])
    by_passage = lax.dot_general(own_columns, queries, contract_rows, preferred_element_type=jnp.float32)
    passage_grad = logit_scale * (by_passage[:q_count] - by_passage[q_count:])

    reduced_activation = jnp.dot(
        token_rows, adapter_down_weight, preferred_element_type=jnp.float32
    ).astype(jnp.bfloat16)
    hidden_state = (
        residual_input.reshape(-1, model_width).astype(jnp.float32)
        + jnp.dot(token_rows, full_weight, preferred_element_type=jnp.float32)
        + adapter_scale
        * jnp.dot(reduced_activation, adapter_up_weight, preferred_element_type=jnp.float32)
    )
    row_grads = query_grad[:seq_here]
    position = jnp.arange(seq_len, dtype=jnp.int32)
    weight = (
        grad_scale
        * (position[None, :] < lengths[:, None]).astype(jnp.float32)
        / lengths[:, None].astype(jnp.float32)
    )
    gained = (
        weight[:, :, None] * row_grads[:, None, :] * final_norm_weight[None, None, :]
    ).reshape(-1, model_width)
    inv_rms = lax.rsqrt(jnp.mean(hidden_state * hidden_state, axis=1) + epsilon)
    hidden_grad = (
        inv_rms[:, None] * gained
        - hidden_state
        * (inv_rms * inv_rms * inv_rms * jnp.mean(gained * hidden_state, axis=1))[:, None]
    )
    gradient_portion = hidden_grad.astype(jnp.bfloat16)
    reduced_gradient = (
        adapter_scale
        * lax.dot_general(
            gradient_portion,
            adapter_up_weight,
            contracted_columns,
            preferred_element_type=jnp.float32,
        )
    ).astype(jnp.bfloat16)
    down_part = lax.dot_general(
        reduced_gradient, token_rows, contract_rows, preferred_element_type=jnp.float32
    )
    up_part = adapter_scale * lax.dot_general(
        reduced_activation, gradient_portion, contract_rows, preferred_element_type=jnp.float32
    )
    both = jnp.concatenate([down_part.reshape(-1, 128), up_part.reshape(-1, 128)], axis=0)
    summed = sum_all(groups, shards, both.reshape(groups, shards, -1, 128)).reshape(-1, 128)
    summed = summed / (seq_here * device_count)
    down_rows = rank * heads_width // 128
    down_total = summed[:down_rows].reshape(rank, heads_width).T
    up_total = summed[down_rows:].reshape(rank, model_width)
    head_gradient = (
        lax.dot_general(
            gradient_portion, full_weight, contracted_columns, preferred_element_type=jnp.float32
        )
        + lax.dot_general(
            reduced_gradient,
            adapter_down_weight,
            contracted_columns,
            preferred_element_type=jnp.float32,
        )
    ).astype(jnp.bfloat16)
    return (
        loss,
        scale_grad,
        query_grad,
        passage_grad,
        head_gradient.reshape(seq_here, seq_len, heads_width),
        gradient_portion.reshape(seq_here, seq_len, model_width),
        down_total,
        up_total,
    )


def solution(mesh):
    both = ("group", "fsdp")
    placed = (
        P(both, None),
        P(both, None),
        P(both),
        P(),
        P(both, None, None),
        P(both, None, None),
        P("fsdp", None),
        P(),
        P(),
        P(),
        P(both),
    )
    return jax.shard_map(
        functools.partial(on_device, mesh.shape["group"], mesh.shape["fsdp"]),
        mesh=mesh,
        in_specs=placed,
        out_specs=(
            P(),
            P(),
            P(both, None),
            P(both, None),
            P(both, None, None),
            P(both, None, None),
            P(),
            P(),
        ),
        check_vma=False,
    )
```

time: 599 us -> 379 us (0.63)
  waiting for transfers between devices: 409 us -> 0 us
  Pallas kernels: 0 us -> 290 us
  blocking collectives: 88.8 us -> 0 us
  between operations: 20.4 us -> 5.74 us
  starting transfers between devices: 10.2 us -> 0 us
  matrix products: 43.3 us -> 51.7 us
  local copies, waits for them, and re-layouts: 12 us -> 19.8 us
    pallas_call x0 -> x2, Pallas kernels: none -> 290 us  [the longest x1 263 us: gather_all(): pl.pallas_call(functools.partial(gather_kernel, groups, shards), out_shap...]
    psum x1 -> x0, waiting for transfers between devices: 149 us -> none  [on_device(): lax.psum((down_part, up_weight_partial), ('group', 'fsdp'))]
    reduce_scatter x1 -> x0, waiting for transfers between devices: 108 us -> none  [on_device(): lax.psum_scatter(jnp.dot(my_columns, output_weight, preferred_element_typ...]
    all_gather x3 -> x0, waiting for transfers between devices: 103 us -> none  [the longest x1 70.9 us: on_device(): lax.all_gather(gradient_portion, 'fsdp', axis=0, tiled=True)]
    all_to_all x2 -> x0, waiting for transfers between devices: 47.6 us -> none  [the longest x1 47.6 us: on_device(): lax.all_to_all(token_rows, 'fsdp', split_axis=1, concat_axis=0, tiled=True)]
    psum x1 -> x0, blocking collectives: 46.6 us -> none  [on_device(): lax.psum((loss_part, scale_part), ('group', 'fsdp'))]
    unnamed x1 -> x0, blocking collectives: 42.2 us -> none
    all_to_all x2 -> x0, starting transfers between devices: 9.99 us -> none  [the longest x1 5.42 us: on_device(): lax.all_to_all(token_rows, 'fsdp', split_axis=1, concat_axis=0, tiled=True)]
  transfers between devices with their start and end apart: 7 -> 0, of which waited for: 5 -> 0; matrix products, arithmetic and copies ran while one was open for 7% -> 0% of each run, Pallas kernels for 0% -> 0%
where the time goes in v1:
time: 379 us
  Pallas kernels  290 us (77%)
  matrix products  51.7 us (14%)
  local copies, waits for them, and re-layouts  19.8 us (5%)
  other arithmetic  11.5 us (3%)
  between operations  5.74 us (2%)
    pallas_call x1, Pallas kernels, gather_all(): pl.pallas_call(functools.partial(gather_kernel, groups, shards), out_shap...  263 us
    pallas_call x1, Pallas kernels, sum_all(): pl.pallas_call(functools.partial(sum_kernel, groups, shards), out_shape=j...  26.8 us
    dot_general x1, matrix products, on_device(): jnp.dot(token_rows, full_weight, preferred_element_type=jnp.float32)  18.7 us
    dot_general x1, matrix products, on_device(): lax.dot_general(gradient_portion, full_weight, contracted_columns, prefer...  17.6 us
    unnamed x20, local copies, waits for them, and re-layouts  10 us

profile of v1, /device:TPU:1, one launch (start us, length us, event | category | flops | bytes accessed | tf_op | source)
XLA Modules:
  0.0 378.5 jit_solution(9320089745337559646)
XLA Ops:
  0.6 0.8 fusion.30
  2.3 0.8 reshape.143
  3.7 263.1 %gather_all.1 = (bf16[4096,4096]{1,0:T(8,128)(2,1)}, bf16[8,4,16,2176]{3,2,1,0:T(8,128)(2,1)}) custom-call(bf16[1024,4096]{1,0:T(8,128)(2,1)} %own_w.1, bf16[16,2176]{1,0:T(8,128)(2,1)} %maximum_maximum_fusion.own_pair), custom_call_target="tpu_custom_call" | custom-call | tf_op jit(solution)/shard_map/gather_all/pallas_call | solution.py:224
  266.9 3.1 fusion.33
  270.0 1.4 reshape.145
  271.4 2.2 reshape.146
  274.3 1.7 fusion.35
  276.1 0.9 slice.55
  277.5 1.5 fusion.18
  280.0 4.1 %copy.30 = bf16[1,256,4096]{1,2,0:T(8,128)(2,1)} copy(bf16[1,256,4096]{2,1,0:T(8,128)(2,1)} %param.15) | data formatting | bytes 4194304 | tf_op args[4]
  284.1 18.7 %fusion.1 = f32[256,4096]{0,1:T(8,128)} fusion(bf16[4096,4096]{1,0:T(8,128)(2,1)} %get-tuple-element.11, bf16[1,256,4096]{1,2,0:T(8,128)(2,1)} %copy.30, bf16[1,256,4096]{2,1,0:T(8,128)(2,1)S(1)} %copy-done), kind=kOutput, calls=%fused_computation.4 | convolution fusion | flops 8592031744 | bytes 41943040 | tf_op jit(solution)/shard_map/dot_general | solution.py:404
  304.1 4.1 %multiply_reduce_fusion.1 = (f32[256]{0:T(256)S(1)}, f32[256]{0:T(256)S(1)}, f32[256,4096]{0,1:T(8,128)S(1)}) fusion(f32[4096]{0:T(1024)S(1)} %copy-done.7, f32[4096]{0:T(1024)S(1)} %bitcast.68, f32[256]{0:T(256)S(1)} %fusion.27, f32[256,4096]{0,1:T(8,128)} %fusion.1, bf16[256,16]{0,1:T(8,128)(2,1)S(1)} %fusion.10, bf16[16,4096]{1,0:T(8,128)(2,1)S(1)} %copy-done.5), kind=kOutput, calls=%fused_computation.11 | convolution fusion | flops 41942528 | bytes 8563712 | tf_op jit(solution)/shard_map/dot_general | solution.py:406
  308.3 2.3 subtract_convert_fusion
  310.6 1.3 copy-done.2
  312.7 2.2 convolution_multiply_fusion.1
  315.1 0.8 pad_maximum_fusion
  315.9 26.8 %sum_all.1 = f32[8,4,32,128]{3,2,1,0:T(8,128)} custom-call(f32[8,4,32,128]{3,2,1,0:T(8,128)} %bitcast.61), custom_call_target="tpu_custom_call" | custom-call | tf_op jit(solution)/shard_map/sum_all/pallas_call | solution.py:305
  342.6 1.1 broadcast_multiply_fusion
  343.8 0.9 copy.42
  344.6 0.9 copy.43
  345.5 4.2 %fusion.54 = bf16[1,256,4096]{1,2,0:T(8,128)(2,1)S(1)} fusion(f32[256,4096]{0,1:T(8,128)} %copy-done.3, f32[256]{0:T(256)S(1)} %get-tuple-element.48, f32[4096]{0:T(1024)S(1)} %copy-done.7, f32[4096]{0:T(1024)S(1)} %bitcast.70, f32[256]{0:T(256)S(1)} %fusion.27, f32[256]{0:T(256)S(1)} %get-tuple-element.47), kind=kLoop, calls=%fused_computation.77 | loop fusion | flops 6291456 | bytes 6327296 | tf_op jit(solution)/shard_map/reshape | solution.py:463
  349.7 2.9 copy.32
  352.6 17.6 %fusion.36 = f32[256,4096]{1,0:T(8,128)} fusion(bf16[256,4096]{0,1:T(8,128)(2,1)} %copy-done.2, bf16[4096,4096]{1,0:T(8,128)(2,1)} %get-tuple-element.11), kind=kOutput, calls=%fused_computation.76 | convolution fusion | flops 8589934592 | bytes 39845888 | tf_op jit(solution)/shard_map/dot_general | solution.py:447
  370.1 4.2 %fusion.3 = bf16[1,256,4096]{2,1,0:T(8,128)(2,1)} fusion(f32[256,4096]{1,0:T(8,128)} %fusion.36, bf16[256,16]{0,1:T(8,128)(2,1)S(1)} %fusion.9, bf16[4096,16]{0,1:T(8,128)(2,1)S(1)} %copy-done.4), kind=kOutput, calls=%fused_computation.6 | convolution fusion | flops 35651584 | bytes 6430720 | tf_op jit(solution)/shard_map/dot_general | solution.py:450
  (44 shorter events, 5.3 us)
Async XLA Ops:
  0.6 283.4 %copy-start = (bf16[1,256,4096]{2,1,0:T(8,128)(2,1)S(1)}, bf16[1,256,4096]{2,1,0:T(8,128)(2,1)}, u32[]{:S(2)}) copy-start(bf16[1,256,4096]{2,1,0:T(8,128)(2,1)} %param.16) | copy-start | bytes 6291460
  280.0 22.8 %copy-start.6 = (f32[4,4096]{1,0:T(4,128)}, f32[4,4096]{1,0:T(4,128)S(1)}, u32[]{:S(2)}) copy-start(f32[4,4096]{1,0:T(4,128)S(1)} %get-tuple-element.55) | copy-start | bytes 196612
  284.1 19.4 %copy-start.4 = (bf16[4096,16]{0,1:T(8,128)(2,1)S(1)}, bf16[4096,16]{0,1:T(8,128)(2,1)}, u32[]{:S(2)}) copy-start(bf16[4096,16]{0,1:T(8,128)(2,1)} %param.18) | copy-start | bytes 393220
  284.1 20.0 %copy-start.5 = (bf16[16,4096]{1,0:T(8,128)(2,1)S(1)}, bf16[16,4096]{1,0:T(8,128)(2,1)}, u32[]{:S(2)}) copy-start(bf16[16,4096]{1,0:T(8,128)(2,1)} %param.19) | copy-start | bytes 393220
  284.1 20.1 %copy-start.7 = (f32[4096]{0:T(1024)S(1)}, f32[4096]{0:T(1024)}, u32[]{:S(2)}) copy-start(f32[4096]{0:T(1024)} %param.20) | copy-start | bytes 49156
  308.3 4.0 %copy-start.3 = (f32[256,4096]{0,1:T(8,128)}, f32[256,4096]{0,1:T(8,128)S(1)}, u32[]{:S(2)}) copy-start(f32[256,4096]{0,1:T(8,128)S(1)} %get-tuple-element.53) | copy-start | bytes 12582916
  310.6 1.3 copy-start.2
  352.6 23.7 %copy-start.1 = (bf16[1,256,4096]{2,1,0:T(8,128)(2,1)S(1)}, bf16[1,256,4096]{2,1,0:T(8,128)(2,1)}, u32[]{:S(2)}) copy-start(bf16[1,256,4096]{2,1,0:T(8,128)(2,1)} %param.16) | copy-start | bytes 6291460

commit v2 on v1

--- a/solution.py
+++ b/solution.py
@@ -32,7 +32,7 @@
 def gather_kernel(
     groups, shards, own_w, own_pair, w_all, pair_all,
     local_sem, z_send, z_recv, pz_send, pz_recv,
-    ring_send, ring_recv, sib_send, sib_recv,
+    ring_send, ring_recv, sib_send, sib_recv, staged,
 ):
     g = lax.axis_index("group")
     f = lax.axis_index("fsdp")
@@ -62,85 +62,106 @@
     def half_piece(block, owner, way):
         return w_all.at[pl.ds(pl.multiple_of(block * rows + owner * part + way * half, 16), half)]
 
-    def z_copy(k, side):
+    def quarter(block, owner, way, sub):
+        columns = own_w.shape[1] // 2
+        return w_all.at[
+            pl.ds(pl.multiple_of(block * rows + owner * part + way * half, 16), half),
+            pl.ds(sub * columns, columns),
+        ]
+
+    last = shards - 1
+    near = jnp.minimum(f, last - f)
+    tied = jnp.minimum(near, 1)
+
+    def order(j):
+        paired = (j < 2 * near).astype(jnp.int32)
+        far_side = (f < last - f).astype(jnp.int32)
+        hop = paired * (lax.div(j, 2) + 1) + (1 - paired) * (near + 1 + j - 2 * near)
+        side = paired * lax.rem(j, 2) + (1 - paired) * far_side
+        return hop, side, f - (1 - 2 * side) * hop
+
+    def z_copy(src, block, hop, side):
         step = 1 - 2 * side
-        block = f - step * (k - 1)
-        here = own_w.at[pl.ds(pl.multiple_of(g * part, 16), part)] if k == 1 else piece(block, g)
-        there = (block >= 0) & (block < shards) & (f + step >= 0) & (f + step < shards)
-        return there, remote(
-            here, piece(block, g), z_send.at[side, k - 1], z_recv.at[side, k - 1], (g, f + step)
+        return remote(
+            src, piece(block, g), z_send.at[side, hop - 1], z_recv.at[side, hop - 1], (g, f + step)
         )
 
-    def z_start(k):
-        for side in (0, 1):
-            there, copy = z_copy(k, side)
-
-            @pl.when(there)
-            def _():
-                copy.start()
-
-    def z_wait(k):
-        for side in (0, 1):
-            block = f - (1 - 2 * side) * k
-
-            @pl.when((block >= 0) & (block < shards))
-            def _():
-                remote(
-                    piece(block, g), piece(block, g), z_send.at[side, k - 1], z_recv.at[side, k - 1], sibling
-                ).wait_recv()
-
-    z_start(1)
-    keep_w = pltpu.make_async_copy(
-        own_w, w_all.at[pl.ds(pl.multiple_of(f * rows, 16), rows)], local_sem.at[0]
-    )
-    keep_pair = pltpu.make_async_copy(own_pair, pair_all.at[g, f], local_sem.at[1])
-    keep_pair.start()
+    def on_line(side):
+        onward = f + 1 - 2 * side
+        return (onward >= 0) & (onward < shards)
+
+    def arrive(j):
+        hop, side, block = order(j)
+        z_copy(piece(block, g), block, hop, side).wait_recv()
+
+        @pl.when(on_line(side))
+        def _():
+            z_copy(piece(block, g), block, hop + 1, side).start()
+
     pair_copies = [
         remote(own_pair, pair_all.at[g, f], pz_send.at[k], pz_recv.at[k], (g, lax.rem(f + k, shards)))
         for k in range(1, shards)
     ]
     for copy in pair_copies:
         copy.start()
-    keep_w.start()
+    keep_pair = pltpu.make_async_copy(own_pair, pair_all.at[g, f], local_sem.at[1])
+    keep_pair.start()
+    own_part = own_w.at[pl.ds(pl.multiple_of(g * part, 16), part)]
+    for side in (0, 1):
+
+        @pl.when(on_line(side))
+        def _():
+            z_copy(own_part, f, 1, side).start()
+
+    stage = pltpu.make_async_copy(own_w, staged, local_sem.at[0])
+    stage.start()
     keep_pair.wait()
     for k in range(1, shards):
         source = lax.rem(f + shards - k, shards)
         remote(own_pair, pair_all.at[g, source], pz_send.at[k], pz_recv.at[k], sibling).wait_recv()
 
-    def ring(slot, whole, halves):
-        pieces = []
-        own = remote(whole, whole, sib_send.at[slot, chips - 1, 0], sib_recv.at[slot, chips - 1, 0], sibling)
-        own.start()
+    def ring_copy(slot, h, way, sub, ref):
+        at = 2 * way + sub
+        return remote(ref, ref, ring_send.at[slot, h - 1, at], ring_recv.at[slot, h - 1, at], neighbours[way])
+
+    def from_behind(way, h):
+        return member(place - (1 - 2 * way) * h)
+
+    def own_hand(slot, whole, other):
+        return remote(whole, other, sib_send.at[slot, chips - 1, 0], sib_recv.at[slot, chips - 1, 0], sibling)
+
+    def ring_start(slot, whole, cut, subs):
+        for sub in range(subs):
+            for way in (0, 1):
+                ring_copy(slot, 1, way, sub, cut(from_behind(way, 0), way, sub)).start()
+        own_hand(slot, whole, whole).start()
+
+    def ring(slot, cut, subs, halves, late):
         for h in range(1, chips):
+            if h == chips - 1:
+                late()
+            for sub in range(subs):
+                for way in (0, 1):
+                    got = cut(from_behind(way, h), way, sub)
+                    ring_copy(slot, h, way, sub, got).wait_recv()
+                    if h < chips - 1:
+                        ring_copy(slot, h + 1, way, sub, got).start()
             for way in (0, 1):
-                step = 1 - 2 * way
-                src = halves(member(place - step * (h - 1)), way)
-                remote(
-                    src, src, ring_send.at[slot, h - 1, way], ring_recv.at[slot, h - 1, way], neighbours[way]
-                ).start()
-            for way in (0, 1):
-                step = 1 - 2 * way
-                got = halves(member(place - step * h), way)
-                remote(
-                    got, got, ring_send.at[slot, h - 1, way], ring_recv.at[slot, h - 1, way], neighbours[way]
-                ).wait_recv()
+                got = halves(from_behind(way, h), way)
                 remote(
                     got, got, sib_send.at[slot, h - 1, way], sib_recv.at[slot, h - 1, way], sibling
                 ).start()
 
-    def ring_finish(slot, whole, halves, other_whole, other_halves):
-        own = remote(whole, other_whole, sib_send.at[slot, chips - 1, 0], sib_recv.at[slot, chips - 1, 0], sibling)
+    def ring_finish(slot, whole, cut, subs, halves, other_whole, other_halves):
+        own = own_hand(slot, whole, other_whole)
         own.wait_send()
         own.wait_recv()
         for h in range(1, chips):
             for way in (0, 1):
-                step = 1 - 2 * way
-                sent = halves(member(place - step * (h - 1)), way)
-                remote(
-                    sent, sent, ring_send.at[slot, h - 1, way], ring_recv.at[slot, h - 1, way], neighbours[way]
-                ).wait_send()
-                got = halves(member(place - step * h), way)
-                other = other_halves(member(place - step * h), way)
+                for sub in range(subs):
+                    ring_copy(slot, h, way, sub, cut(from_behind(way, h - 1), way, sub)).wait_send()
+                got = halves(from_behind(way, h), way)
+                other = other_halves(from_behind(way, h), way)
                 handed = remote(
                     got, other, sib_send.at[slot, h - 1, way], sib_recv.at[slot, h - 1, way], sibling
                 )
@@ -149,67 +170,63 @@
 
     middle = shards // 2
 
-    def pair_half(owner, way):
+    def pair_half(owner, way, sub=0):
         return pair_all.at[owner, pl.ds(way * middle, middle)]
 
     def flip(owner):
         return owner + 1 - 2 * core
 
-    ring(shards, pair_all.at[g], pair_half)
-
-    def w_ring(block):
-        ring(block, piece(block, g), lambda owner, way: half_piece(block, owner, way))
-
-    def w_finish(block):
+    def w_start(j):
+        _, _, block = order(j)
+        ring_start(block, piece(block, g), functools.partial(quarter, block), 2)
+
+    ring_start(shards, pair_all.at[g], pair_half, 1)
+    ring(shards, pair_half, 1, pair_half, lambda: None)
+    stage.wait()
+    keep_w = pltpu.make_async_copy(
+        staged, w_all.at[pl.ds(pl.multiple_of(f * rows, 16), rows)], local_sem.at[0]
+    )
+    keep_w.start()
+    arrive(0)
+    if last > 1:
+
+        @pl.when(tied > 0)
+        def _():
+            arrive(1)
+
+    w_start(0)
+    for j in range(last):
+        def late():
+            @pl.when(j + 1 + tied < last)
+            def _():
+                arrive(j + 1 + tied)
+
+            if j + 1 < last:
+                w_start(j + 1)
+
+        _, _, block = order(j)
+        ring(block, functools.partial(quarter, block), 2, functools.partial(half_piece, block), late)
+
+    ring_finish(
+        shards, pair_all.at[g], pair_half, 1, pair_half, pair_all.at[flip(g)],
+        lambda owner, way: pair_half(flip(owner), way),
+    )
+    for side in (0, 1):
+
+        @pl.when(on_line(side))
+        def _():
+            z_copy(own_part, f, 1, side).wait_send()
+
+    for j in range(last):
+        hop, side, block = order(j)
         ring_finish(
-            block,
-            piece(block, g),
-            lambda owner, way: half_piece(block, owner, way),
-            piece(block, flip(g)),
-            lambda owner, way: half_piece(block, flip(owner), way),
+            block, piece(block, g), functools.partial(quarter, block), 2, functools.partial(half_piece, block),
+            piece(block, flip(g)), lambda owner, way: half_piece(block, flip(owner), way),
         )
 
-    def blocks(k):
-        low = (f - k >= 0).astype(jnp.int32)
-        high = (f + k < shards).astype(jnp.int32)
-        first = low * (f - k) + (1 - low) * (f + k)
-        return ((low + high > 0, first), (low + high > 1, f + k))
-
-    z_wait(1)
-    if shards > 2:
-        z_start(2)
-    for k in range(1, shards):
-        first, second = blocks(k)
-
-        @pl.when(first[0])
+        @pl.when(on_line(side))
         def _():
-            w_ring(first[1])
-
-        if k + 1 < shards:
-            z_wait(k + 1)
-        if k + 2 < shards:
-            z_start(k + 2)
-
-        @pl.when(second[0])
-        def _():
-            w_ring(second[1])
-
-    ring_finish(
-        shards, pair_all.at[g], pair_half, pair_all.at[flip(g)], lambda owner, way: pair_half(flip(owner), way)
-    )
-    for k in range(1, shards):
-        for there, block in blocks(k):
-
-            @pl.when(there)
-            def _():
-                w_finish(block)
-
-        for side in (0, 1):
-            there, copy = z_copy(k, side)
-
-            @pl.when(there)
-            def _():
-                copy.wait_send()
+            z_copy(piece(block, g), block, hop + 1, side).wait_send()
 
     for copy in pair_copies:
         copy.wait_send()
@@ -235,12 +252,17 @@
             dma((2, shards)),
             dma((shards,)),
             dma((shards,)),
+            dma((shards + 1, chips, 4)),
+            dma((shards + 1, chips, 4)),
             dma((shards + 1, chips, 2)),
             dma((shards + 1, chips, 2)),
-            dma((shards + 1, chips, 2)),
-            dma((shards + 1, chips, 2)),
+            pltpu.VMEM(own_w.shape, own_w.dtype),
         ],
-        compiler_params=pltpu.CompilerParams(collective_id=0, has_side_effects=True),
+        compiler_params=pltpu.CompilerParams(
+            collective_id=0,
+            has_side_effects=True,
+            vmem_limit_bytes=own_w.size * own_w.dtype.itemsize + (8 << 20),
+        ),
         name="gather_all",
     )(own_w, own_pair)
 

time: 379 us -> 261 us (0.69)
  Pallas kernels: 290 us -> 168 us
    pallas_call x1, Pallas kernels: 263 us -> 142 us  [gather_all(): pl.pallas_call(functools.partial(gather_kernel, groups, shards), out_shap...]
    unnamed x20 -> x24, local copies, waits for them, and re-layouts: 10 us -> 14.8 us
where the time goes in v2:
time: 261 us; the launch traced here: 260 us
  Pallas kernels  168 us (64%)
  matrix products  51.7 us (20%)
  local copies, waits for them, and re-layouts  23 us (9%)
  other arithmetic  11 us (4%)
  between operations  5.76 us (2%)
    pallas_call x1, Pallas kernels, gather_all(): pl.pallas_call(functools.partial(gather_kernel, groups, shards), out_shap...  142 us
    pallas_call x1, Pallas kernels, sum_all(): pl.pallas_call(functools.partial(sum_kernel, groups, shards), out_shape=j...  26.6 us
    dot_general x1, matrix products, on_device(): jnp.dot(token_rows, full_weight, preferred_element_type=jnp.float32)  18.7 us
    dot_general x1, matrix products, on_device(): lax.dot_general(gradient_portion, full_weight, contracted_columns, prefer...  17.6 us
    unnamed x24, local copies, waits for them, and re-layouts  14.8 us

profile of v2, /device:TPU:1, one launch (start us, length us, event | category | flops | bytes accessed | tf_op | source)
XLA Modules:
  0.0 259.7 jit_solution(5566485563036162869)
XLA Ops:
  3.1 3.4 %copy-done.2 = bf16[1024,4096]{1,0:T(8,128)(2,1)S(1)} copy-done((bf16[1024,4096]{1,0:T(8,128)(2,1)S(1)}, bf16[1024,4096]{1,0:T(8,128)(2,1)}, u32[]{:S(2)}) %copy-start.2) | copy-done | bytes 8388632
  6.5 141.6 %gather_all.1 = (bf16[4096,4096]{1,0:T(8,128)(2,1)}, bf16[8,4,16,2176]{3,2,1,0:T(8,128)(2,1)S(1)}) custom-call(bf16[1024,4096]{1,0:T(8,128)(2,1)S(1)} %copy-done.2, bf16[16,2176]{1,0:T(8,128)(2,1)S(1)} %maximum_maximum_fusion.own_pair), custom_call_target="tpu_custom_call" | custom-call | tf_op jit(solution)/shard_map/gather_all/pallas_call | solution.py:241
  148.2 1.4 copy-done.3
  149.5 1.6 fusion.33
  151.1 1.4 reshape.145
  152.5 2.2 reshape.146
  155.4 1.7 fusion.35
  157.2 0.9 slice.55
  158.6 1.5 fusion.18
  161.1 4.1 %copy.30 = bf16[1,256,4096]{1,2,0:T(8,128)(2,1)} copy(bf16[1,256,4096]{2,1,0:T(8,128)(2,1)} %param.15) | data formatting | bytes 4194304 | tf_op args[4]
  165.2 18.7 %fusion.1 = f32[256,4096]{0,1:T(8,128)} fusion(bf16[4096,4096]{1,0:T(8,128)(2,1)} %get-tuple-element.11, bf16[1,256,4096]{1,2,0:T(8,128)(2,1)} %copy.30, bf16[1,256,4096]{2,1,0:T(8,128)(2,1)S(1)} %copy-done), kind=kOutput, calls=%fused_computation.4 | convolution fusion | flops 8592031744 | bytes 41943040 | tf_op jit(solution)/shard_map/dot_general | solution.py:426
  185.3 4.1 %multiply_reduce_fusion.1 = (f32[256]{0:T(256)S(1)}, f32[256]{0:T(256)S(1)}, f32[256,4096]{0,1:T(8,128)S(1)}) fusion(f32[4096]{0:T(1024)S(1)} %copy-done.9, f32[4096]{0:T(1024)S(1)} %bitcast.68, f32[256]{0:T(256)S(1)} %fusion.27, f32[256,4096]{0,1:T(8,128)} %fusion.1, bf16[256,16]{0,1:T(8,128)(2,1)S(1)} %fusion.10, bf16[16,4096]{1,0:T(8,128)(2,1)S(1)} %copy-done.7), kind=kOutput, calls=%fused_computation.11 | convolution fusion | flops 41942528 | bytes 8563712 | tf_op jit(solution)/shard_map/dot_general | solution.py:428
  189.4 2.5 subtract_convert_fusion
  191.9 1.3 copy-done.4
  194.1 2.2 convolution_multiply_fusion.1
  196.4 0.8 pad_maximum_fusion
  197.2 26.6 %sum_all.1 = f32[8,4,32,128]{3,2,1,0:T(8,128)} custom-call(f32[8,4,32,128]{3,2,1,0:T(8,128)} %bitcast.63), custom_call_target="tpu_custom_call" | custom-call | tf_op jit(solution)/shard_map/sum_all/pallas_call | solution.py:327
  223.8 1.1 broadcast_multiply_fusion
  224.9 0.9 copy.42
  225.8 0.9 copy.43
  226.6 4.2 %fusion.54 = bf16[1,256,4096]{1,2,0:T(8,128)(2,1)S(1)} fusion(f32[256,4096]{0,1:T(8,128)} %copy-done.5, f32[256]{0:T(256)S(1)} %get-tuple-element.48, f32[4096]{0:T(1024)S(1)} %copy-done.9, f32[4096]{0:T(1024)S(1)} %bitcast.70, f32[256]{0:T(256)S(1)} %fusion.27, f32[256]{0:T(256)S(1)} %get-tuple-element.47), kind=kLoop, calls=%fused_computation.77 | loop fusion | flops 6291456 | bytes 6327296 | tf_op jit(solution)/shard_map/reshape | solution.py:485
  230.8 2.9 %copy.32 = bf16[1,256,4096]{2,1,0:T(8,128)(2,1)} copy(bf16[1,256,4096]{1,2,0:T(8,128)(2,1)S(1)} %fusion.54) | data formatting | bytes 4194304
  233.7 17.6 %fusion.36 = f32[256,4096]{1,0:T(8,128)} fusion(bf16[256,4096]{0,1:T(8,128)(2,1)} %copy-done.4, bf16[4096,4096]{1,0:T(8,128)(2,1)} %get-tuple-element.11), kind=kOutput, calls=%fused_computation.76 | convolution fusion | flops 8589934592 | bytes 39845888 | tf_op jit(solution)/shard_map/dot_general | solution.py:469
  251.3 4.2 %fusion.3 = bf16[1,256,4096]{2,1,0:T(8,128)(2,1)} fusion(f32[256,4096]{1,0:T(8,128)} %fusion.36, bf16[256,16]{0,1:T(8,128)(2,1)S(1)} %fusion.9, bf16[4096,16]{0,1:T(8,128)(2,1)S(1)} %copy-done.6), kind=kOutput, calls=%fused_computation.6 | convolution fusion | flops 35651584 | bytes 6430720 | tf_op jit(solution)/shard_map/dot_general | solution.py:472
  (48 shorter events, 6.3 us)
Async XLA Ops:
  0.6 164.6 %copy-start = (bf16[1,256,4096]{2,1,0:T(8,128)(2,1)S(1)}, bf16[1,256,4096]{2,1,0:T(8,128)(2,1)}, u32[]{:S(2)}) copy-start(bf16[1,256,4096]{2,1,0:T(8,128)(2,1)} %param.16) | copy-start | bytes 6291460
  3.1 3.4 %copy-start.2 = (bf16[1024,4096]{1,0:T(8,128)(2,1)S(1)}, bf16[1024,4096]{1,0:T(8,128)(2,1)}, u32[]{:S(2)}) copy-start(bf16[1024,4096]{1,0:T(8,128)(2,1)} %own_w.1) | copy-start | bytes 25165828
  148.1 1.4 copy-start.3
  161.1 22.8 %copy-start.8 = (f32[4,4096]{1,0:T(4,128)}, f32[4,4096]{1,0:T(4,128)S(1)}, u32[]{:S(2)}) copy-start(f32[4,4096]{1,0:T(4,128)S(1)} %get-tuple-element.55) | copy-start | bytes 196612
  165.2 19.4 %copy-start.6 = (bf16[4096,16]{0,1:T(8,128)(2,1)S(1)}, bf16[4096,16]{0,1:T(8,128)(2,1)}, u32[]{:S(2)}) copy-start(bf16[4096,16]{0,1:T(8,128)(2,1)} %param.18) | copy-start | bytes 393220
  165.2 20.0 %copy-start.7 = (bf16[16,4096]{1,0:T(8,128)(2,1)S(1)}, bf16[16,4096]{1,0:T(8,128)(2,1)}, u32[]{:S(2)}) copy-start(bf16[16,4096]{1,0:T(8,128)(2,1)} %param.19) | copy-start | bytes 393220
  165.2 20.1 %copy-start.9 = (f32[4096]{0:T(1024)S(1)}, f32[4096]{0:T(1024)}, u32[]{:S(2)}) copy-start(f32[4096]{0:T(1024)} %param.20) | copy-start | bytes 49156
  189.4 4.2 %copy-start.5 = (f32[256,4096]{0,1:T(8,128)}, f32[256,4096]{0,1:T(8,128)S(1)}, u32[]{:S(2)}) copy-start(f32[256,4096]{0,1:T(8,128)S(1)} %get-tuple-element.53) | copy-start | bytes 12582916
  191.9 1.3 copy-start.4
  233.7 23.7 %copy-start.1 = (bf16[1,256,4096]{2,1,0:T(8,128)(2,1)S(1)}, bf16[1,256,4096]{2,1,0:T(8,128)(2,1)}, u32[]{:S(2)}) copy-start(bf16[1,256,4096]{2,1,0:T(8,128)(2,1)} %param.16) | copy-start | bytes 6291460

commit v3 on v2

--- a/solution.py
+++ b/solution.py
@@ -80,23 +80,30 @@
         side = paired * lax.rem(j, 2) + (1 - paired) * far_side
         return hop, side, f - (1 - 2 * side) * hop
 
-    def z_copy(src, block, hop, side):
+    def z_piece(block, sub):
+        columns = own_w.shape[1] // 2
+        return w_all.at[
+            pl.ds(pl.multiple_of(block * rows + g * part, 16), part), pl.ds(sub * columns, columns)
+        ]
+
+    def z_copy(src, block, hop, side, sub):
         step = 1 - 2 * side
+        at = 2 * (hop - 1) + sub
         return remote(
-            src, piece(block, g), z_send.at[side, hop - 1], z_recv.at[side, hop - 1], (g, f + step)
+            src, z_piece(block, sub), z_send.at[side, at], z_recv.at[side, at], (g, f + step)
         )
 
     def on_line(side):
         onward = f + 1 - 2 * side
         return (onward >= 0) & (onward < shards)
 
-    def arrive(j):
+    def arrive(j, sub):
         hop, side, block = order(j)
-        z_copy(piece(block, g), block, hop, side).wait_recv()
+        z_copy(z_piece(block, sub), block, hop, side, sub).wait_recv()
 
         @pl.when(on_line(side))
         def _():
-            z_copy(piece(block, g), block, hop + 1, side).start()
+            z_copy(z_piece(block, sub), block, hop + 1, side, sub).start()
 
     pair_copies = [
         remote(own_pair, pair_all.at[g, f], pz_send.at[k], pz_recv.at[k], (g, lax.rem(f + k, shards)))
@@ -106,13 +113,19 @@
         copy.start()
     keep_pair = pltpu.make_async_copy(own_pair, pair_all.at[g, f], local_sem.at[1])
     keep_pair.start()
-    own_part = own_w.at[pl.ds(pl.multiple_of(g * part, 16), part)]
-    for side in (0, 1):
-
-        @pl.when(on_line(side))
-        def _():
-            z_copy(own_part, f, 1, side).start()
-
+
+    def own_part(sub):
+        columns = own_w.shape[1] // 2
+        return own_w.at[pl.ds(pl.multiple_of(g * part, 16), part), pl.ds(sub * columns, columns)]
+
+    def z_first(sub):
+        for side in (0, 1):
+
+            @pl.when(on_line(side))
+            def _():
+                z_copy(own_part(sub), f, 1, side, sub).start()
+
+    z_first(0)
     stage = pltpu.make_async_copy(own_w, staged, local_sem.at[0])
     stage.start()
     keep_pair.wait()
@@ -120,6 +133,8 @@
         source = lax.rem(f + shards - k, shards)
         remote(own_pair, pair_all.at[g, source], pz_send.at[k], pz_recv.at[k], sibling).wait_recv()
 
+    z_first(1)
+
     def ring_copy(slot, h, way, sub, ref):
         at = 2 * way + sub
         return remote(ref, ref, ring_send.at[slot, h - 1, at], ring_recv.at[slot, h - 1, at], neighbours[way])
@@ -130,8 +145,9 @@
     def own_hand(slot, whole, other):
         return remote(whole, other, sib_send.at[slot, chips - 1, 0], sib_recv.at[slot, chips - 1, 0], sibling)
 
-    def ring_start(slot, whole, cut, subs):
+    def ring_start(slot, whole, cut, subs, ready=lambda sub: None):
         for sub in range(subs):
+            ready(sub)
             for way in (0, 1):
                 ring_copy(slot, 1, way, sub, cut(from_behind(way, 0), way, sub)).start()
         own_hand(slot, whole, whole).start()
@@ -176,9 +192,9 @@
     def flip(owner):
         return owner + 1 - 2 * core
 
-    def w_start(j):
+    def w_start(j, ready=lambda sub: None):
         _, _, block = order(j)
-        ring_start(block, piece(block, g), functools.partial(quarter, block), 2)
+        ring_start(block, piece(block, g), functools.partial(quarter, block), 2, ready)
 
     ring_start(shards, pair_all.at[g], pair_half, 1)
     ring(shards, pair_half, 1, pair_half, lambda: None)
@@ -187,19 +203,22 @@
         staged, w_all.at[pl.ds(pl.multiple_of(f * rows, 16), rows)], local_sem.at[0]
     )
     keep_w.start()
-    arrive(0)
-    if last > 1:
-
-        @pl.when(tied > 0)
-        def _():
-            arrive(1)
-
-    w_start(0)
+
+    def ready(sub):
+        arrive(0, sub)
+        if last > 1:
+
+            @pl.when(tied > 0)
+            def _():
+                arrive(1, sub)
+
+    w_start(0, ready)
     for j in range(last):
         def late():
             @pl.when(j + 1 + tied < last)
             def _():
-                arrive(j + 1 + tied)
+                for sub in (0, 1):
+                    arrive(j + 1 + tied, sub)
 
             if j + 1 < last:
                 w_start(j + 1)
@@ -215,7 +234,8 @@
 
         @pl.when(on_line(side))
         def _():
-            z_copy(own_part, f, 1, side).wait_send()
+            for sub in (0, 1):
+                z_copy(own_part(sub), f, 1, side, sub).wait_send()
 
     for j in range(last):
         hop, side, block = order(j)
@@ -226,7 +246,8 @@
 
         @pl.when(on_line(side))
         def _():
-            z_copy(piece(block, g), block, hop + 1, side).wait_send()
+            for sub in (0, 1):
+                z_copy(z_piece(block, sub), block, hop + 1, side, sub).wait_send()
 
     for copy in pair_copies:
         copy.wait_send()
@@ -248,8 +269,8 @@
         out_specs=(any_space, any_space),
         scratch_shapes=[
             dma((2,)),
-            dma((2, shards)),
-            dma((2, shards)),
+            dma((2, 2 * shards)),
+            dma((2, 2 * shards)),
             dma((shards,)),
             dma((shards,)),
             dma((shards + 1, chips, 4)),

time: 261 us -> 255 us (0.977)
  Pallas kernels: 168 us -> 163 us
    pallas_call x1, Pallas kernels: 142 us -> 136 us  [gather_all(): pl.pallas_call(functools.partial(gather_kernel, groups, shards), out_shap...]
where the time goes in v3:
time: 255 us; the launch traced here: 254 us
  Pallas kernels  163 us (64%)
  matrix products  51.7 us (20%)
  local copies, waits for them, and re-layouts  23 us (9%)
  other arithmetic  10.8 us (4%)
  between operations  5.76 us (2%)
    pallas_call x1, Pallas kernels, gather_all(): pl.pallas_call(functools.partial(gather_kernel, groups, shards), out_shap...  136 us
    pallas_call x1, Pallas kernels, sum_all(): pl.pallas_call(functools.partial(sum_kernel, groups, shards), out_shape=j...  26.6 us
    dot_general x1, matrix products, on_device(): jnp.dot(token_rows, full_weight, preferred_element_type=jnp.float32)  18.7 us
    dot_general x1, matrix products, on_device(): lax.dot_general(gradient_portion, full_weight, contracted_columns, prefer...  17.6 us
    unnamed x24, local copies, waits for them, and re-layouts  14.8 us

profile of v3, /device:TPU:1, one launch (start us, length us, event | category | flops | bytes accessed | tf_op | source)
XLA Modules:
  0.0 254.0 jit_solution(10975250451905108652)
XLA Ops:
  3.1 3.4 %copy-done.2 = bf16[1024,4096]{1,0:T(8,128)(2,1)S(1)} copy-done((bf16[1024,4096]{1,0:T(8,128)(2,1)S(1)}, bf16[1024,4096]{1,0:T(8,128)(2,1)}, u32[]{:S(2)}) %copy-start.2) | copy-done | bytes 8388632
  6.5 136.2 %gather_all.1 = (bf16[4096,4096]{1,0:T(8,128)(2,1)}, bf16[8,4,16,2176]{3,2,1,0:T(8,128)(2,1)S(1)}) custom-call(bf16[1024,4096]{1,0:T(8,128)(2,1)S(1)} %copy-done.2, bf16[16,2176]{1,0:T(8,128)(2,1)S(1)} %maximum_maximum_fusion.own_pair), custom_call_target="tpu_custom_call" | custom-call | tf_op jit(solution)/shard_map/gather_all/pallas_call | solution.py:262
  142.7 1.4 copy-done.3
  144.0 1.6 fusion.33
  145.6 1.4 reshape.145
  147.1 2.2 reshape.146
  150.0 1.7 fusion.35
  151.7 0.9 slice.55
  153.2 1.5 fusion.18
  155.6 4.1 %copy.30 = bf16[1,256,4096]{1,2,0:T(8,128)(2,1)} copy(bf16[1,256,4096]{2,1,0:T(8,128)(2,1)} %param.15) | data formatting | bytes 4194304 | tf_op args[4]
  159.7 18.7 %fusion.1 = f32[256,4096]{0,1:T(8,128)} fusion(bf16[4096,4096]{1,0:T(8,128)(2,1)} %get-tuple-element.11, bf16[1,256,4096]{1,2,0:T(8,128)(2,1)} %copy.30, bf16[1,256,4096]{2,1,0:T(8,128)(2,1)S(1)} %copy-done), kind=kOutput, calls=%fused_computation.4 | convolution fusion | flops 8592031744 | bytes 41943040 | tf_op jit(solution)/shard_map/dot_general | solution.py:447
  179.8 4.1 %multiply_reduce_fusion.1 = (f32[256]{0:T(256)S(1)}, f32[256]{0:T(256)S(1)}, f32[256,4096]{0,1:T(8,128)S(1)}) fusion(f32[4096]{0:T(1024)S(1)} %copy-done.9, f32[4096]{0:T(1024)S(1)} %bitcast.68, f32[256]{0:T(256)S(1)} %fusion.27, f32[256,4096]{0,1:T(8,128)} %fusion.1, bf16[256,16]{0,1:T(8,128)(2,1)S(1)} %fusion.10, bf16[16,4096]{1,0:T(8,128)(2,1)S(1)} %copy-done.7), kind=kOutput, calls=%fused_computation.11 | convolution fusion | flops 41942528 | bytes 8563712 | tf_op jit(solution)/shard_map/dot_general | solution.py:449
  183.9 2.3 subtract_convert_fusion
  186.3 1.3 copy-done.4
  188.4 2.2 convolution_multiply_fusion.1
  190.7 0.8 pad_maximum_fusion
  191.5 26.6 %sum_all.1 = f32[8,4,32,128]{3,2,1,0:T(8,128)} custom-call(f32[8,4,32,128]{3,2,1,0:T(8,128)} %bitcast.63), custom_call_target="tpu_custom_call" | custom-call | tf_op jit(solution)/shard_map/sum_all/pallas_call | solution.py:348
  218.1 1.1 broadcast_multiply_fusion
  219.3 0.9 copy.42
  220.1 0.9 copy.43
  221.0 4.2 %fusion.54 = bf16[1,256,4096]{1,2,0:T(8,128)(2,1)S(1)} fusion(f32[256,4096]{0,1:T(8,128)} %copy-done.5, f32[256]{0:T(256)S(1)} %get-tuple-element.48, f32[4096]{0:T(1024)S(1)} %copy-done.9, f32[4096]{0:T(1024)S(1)} %bitcast.70, f32[256]{0:T(256)S(1)} %fusion.27, f32[256]{0:T(256)S(1)} %get-tuple-element.47), kind=kLoop, calls=%fused_computation.77 | loop fusion | flops 6291456 | bytes 6327296 | tf_op jit(solution)/shard_map/reshape | solution.py:506
  225.2 2.9 %copy.32 = bf16[1,256,4096]{2,1,0:T(8,128)(2,1)} copy(bf16[1,256,4096]{1,2,0:T(8,128)(2,1)S(1)} %fusion.54) | data formatting | bytes 4194304
  228.1 17.6 %fusion.36 = f32[256,4096]{1,0:T(8,128)} fusion(bf16[256,4096]{0,1:T(8,128)(2,1)} %copy-done.4, bf16[4096,4096]{1,0:T(8,128)(2,1)} %get-tuple-element.11), kind=kOutput, calls=%fused_computation.76 | convolution fusion | flops 8589934592 | bytes 39845888 | tf_op jit(solution)/shard_map/dot_general | solution.py:490
  245.6 4.2 %fusion.3 = bf16[1,256,4096]{2,1,0:T(8,128)(2,1)} fusion(f32[256,4096]{1,0:T(8,128)} %fusion.36, bf16[256,16]{0,1:T(8,128)(2,1)S(1)} %fusion.9, bf16[4096,16]{0,1:T(8,128)(2,1)S(1)} %copy-done.6), kind=kOutput, calls=%fused_computation.6 | convolution fusion | flops 35651584 | bytes 6430720 | tf_op jit(solution)/shard_map/dot_general | solution.py:493
  (48 shorter events, 6.3 us)
Async XLA Ops:
  0.6 159.1 %copy-start = (bf16[1,256,4096]{2,1,0:T(8,128)(2,1)S(1)}, bf16[1,256,4096]{2,1,0:T(8,128)(2,1)}, u32[]{:S(2)}) copy-start(bf16[1,256,4096]{2,1,0:T(8,128)(2,1)} %param.16) | copy-start | bytes 6291460
  3.1 3.4 %copy-start.2 = (bf16[1024,4096]{1,0:T(8,128)(2,1)S(1)}, bf16[1024,4096]{1,0:T(8,128)(2,1)}, u32[]{:S(2)}) copy-start(bf16[1024,4096]{1,0:T(8,128)(2,1)} %own_w.1) | copy-start | bytes 25165828
  142.7 1.4 copy-start.3
  155.6 22.8 %copy-start.8 = (f32[4,4096]{1,0:T(4,128)}, f32[4,4096]{1,0:T(4,128)S(1)}, u32[]{:S(2)}) copy-start(f32[4,4096]{1,0:T(4,128)S(1)} %get-tuple-element.55) | copy-start | bytes 196612
  159.7 19.4 %copy-start.6 = (bf16[4096,16]{0,1:T(8,128)(2,1)S(1)}, bf16[4096,16]{0,1:T(8,128)(2,1)}, u32[]{:S(2)}) copy-start(bf16[4096,16]{0,1:T(8,128)(2,1)} %param.18) | copy-start | bytes 393220
  159.7 20.0 %copy-start.7 = (bf16[16,4096]{1,0:T(8,128)(2,1)S(1)}, bf16[16,4096]{1,0:T(8,128)(2,1)}, u32[]{:S(2)}) copy-start(bf16[16,4096]{1,0:T(8,128)(2,1)} %param.19) | copy-start | bytes 393220
  159.7 20.0 %copy-start.9 = (f32[4096]{0:T(1024)S(1)}, f32[4096]{0:T(1024)}, u32[]{:S(2)}) copy-start(f32[4096]{0:T(1024)} %param.20) | copy-start | bytes 49156
  183.9 4.0 %copy-start.5 = (f32[256,4096]{0,1:T(8,128)}, f32[256,4096]{0,1:T(8,128)S(1)}, u32[]{:S(2)}) copy-start(f32[256,4096]{0,1:T(8,128)S(1)} %get-tuple-element.53) | copy-start | bytes 12582916
  186.2 1.3 copy-start.4
  228.0 23.7 %copy-start.1 = (bf16[1,256,4096]{2,1,0:T(8,128)(2,1)S(1)}, bf16[1,256,4096]{2,1,0:T(8,128)(2,1)}, u32[]{:S(2)}) copy-start(bf16[1,256,4096]{2,1,0:T(8,128)(2,1)} %param.16) | copy-start | bytes 6291460
